TPU v7x, 32 devices: a whole 2x2x4 slice. The times are simulated.
32 devices in a mesh: img: 8 (over y, x, core), txt: 4 (over z).
Axes of the slice: x: 2, y: 2, z: 4, core: 2. Of those that a mesh axis runs over, the one named last changes fastest.
Arguments:
- images: bfloat16 [768, 512], P('img'), may hold values from -1 to 1
- texts: bfloat16 [768, 512], P(('txt', 'img')), may hold values from -1 to 1
Outputs:
- grad_images: float32 [768, 512], P(('img', 'txt'))
- grad_texts: float32 [768, 512], P(('txt', 'img'))
All inputs are finite; a program needn't handle non-finite values.
Results may differ from a plain program's by a relative error of at most 0.0075.
Values may be sent and summed in bfloat16 or wider, within the bound.
A program may use at most 64 MiB of HBM per device.

v0:
```python
import jax
import jax.numpy as jnp
from jax import lax
from jax.experimental import pallas as pl
from jax.experimental.pallas import tpu as pltpu
from jax.sharding import PartitionSpec as P

ROUNDS = 3


logit_scale = 30.0
mix_weight = 0.5
norm_eps = 1e-06
highest = lax.Precision.HIGHEST


def normalize(values):
    wide = values.astype(jnp.float32)
    length = jnp.sqrt(jnp.sum(wide * wide, axis=1, keepdims=True) + norm_eps)
    return (wide / length, length)


def project_back(grad, unit, length):
    along = jnp.sum(unit * grad, axis=1, keepdims=True)
    return (grad - unit * along) / length


def shards(images, texts):
    own_rows = texts.shape[0]
    img_block = images.shape[0]
    img_index = lax.axis_index("img")
    txt_index = lax.axis_index("txt")
    unit_img, len_img = normalize(images)
    img_bf = unit_img.astype(jnp.bfloat16)
    unit_txt, len_txt = normalize(texts)
    txt_bf = lax.all_gather(unit_txt.astype(jnp.bfloat16), "img", axis=0, tiled=True)
    txt_block = txt_bf.shape[0]
    total = float(img_block * lax.axis_size("img"))
    scores = logit_scale * lax.dot_general(
        img_bf, txt_bf, (((1,), (1,)), ((), ())), preferred_element_type=jnp.float32
    )
    kernel = jnp.exp(scores - logit_scale)
    row_weight = jnp.ones((img_block,), jnp.float32)
    col_scale = jnp.ones((txt_block,), jnp.float32)
    col_total = col_scale
    row_total = row_weight
    last_cols = col_scale
    for step in range(ROUNDS + 1):
        col_part = jnp.dot(row_weight, kernel, precision=highest)
        col_sum = lax.psum(col_part, "img")
        if step == 0:
            col_total = col_sum
        if step == ROUNDS:
            last_cols = col_sum
        else:
            col_scale = 1.0 / (total * col_sum)
            row_part = jnp.dot(kernel, col_scale, precision=highest)
            if step == 0:
                stats = jnp.stack([row_part, jnp.sum(kernel, axis=1)])
            else:
                stats = row_part[None, :]
            summed = lax.psum(stats, "txt")
            if step == 0:
                row_total = summed[1]
            row_weight = 1.0 / (total * summed[0])
    col_weight = 1.0 - mix_weight + mix_weight * total * col_scale * last_cols
    img_ids = img_index * img_block + jnp.arange(img_block, dtype=jnp.int32)
    txt_ids = txt_index * txt_block + jnp.arange(txt_block, dtype=jnp.int32)
    eye = (img_ids[:, None] == txt_ids[None, :]).astype(jnp.float32)
    target = (1.0 - mix_weight) * eye + mix_weight * total * row_weight[
        :, None
    ] * kernel * col_scale[None, :]
    grad_logit = 0.5 * (
        kernel / row_total[:, None]
        + col_weight[None, :] * kernel / col_total[None, :]
        - 2.0 * target
    )
    grad_logit = grad_logit.astype(jnp.bfloat16)
    g_img = lax.psum_scatter(
        logit_scale * jnp.dot(grad_logit, txt_bf, preferred_element_type=jnp.float32),
        "txt",
        scatter_dimension=0,
        tiled=True,
    )
    g_txt = lax.psum_scatter(
        logit_scale
        * lax.dot_general(
            grad_logit, img_bf, (((0,), (0,)), ((), ())), preferred_element_type=jnp.float32
        ),
        "img",
        scatter_dimension=0,
        tiled=True,
    )
    own_unit = lax.dynamic_slice_in_dim(unit_img, txt_index * own_rows, own_rows, 0)
    own_len = lax.dynamic_slice_in_dim(len_img, txt_index * own_rows, own_rows, 0)
    grad_images = project_back(g_img, own_unit, own_len)
    grad_texts = project_back(g_txt, unit_txt, len_txt)
    return (grad_images, grad_texts)


MESH = pl.DeviceIdType.MESH
F32 = jnp.float32
BF16 = jnp.bfloat16


def nt_dot(left, right):
    return lax.dot_general(
        left, right, (((1,), (1,)), ((), ())), preferred_element_type=F32
    )


def scaled_kernel(left, right):
    return jnp.exp(logit_scale * nt_dot(left, right) - logit_scale)


def fold_rows(values):
    rows, cols = values.shape
    return jnp.sum(values.reshape(rows // 8, 8, cols), axis=0)


def gathered_body(
    images_ref,
    texts_ref,
    gimg_ref,
    gtxt_ref,
    img_buf,
    txt_buf,
    col_in,
    wide_img,
    raw_img,
    raw_txt,
    kt,
    first_scale,
    send_sem,
    img_recv,
    txt_recv,
    col_recv,
    load_sem,
):
    slots, slot_rows, width = img_buf.shape
    depth, own = col_in.shape[0], texts_ref.shape[0]
    half = width // 2
    total_rows = slots * slot_rows
    chunks = img_recv.shape[1]
    piece = slot_rows // chunks

    load_txt = pltpu.make_async_copy(texts_ref, raw_txt, load_sem.at[0])
    load_txt.start()
    load_img = pltpu.make_async_copy(images_ref, raw_img, load_sem.at[1])
    load_img.start()

    me = lax.axis_index("img")
    layer = lax.axis_index("txt")
    core = me % 2
    x = (me // 2) % 2
    y = me // 4
    first = (y + core * (1 - 2 * y)) * 4 + (x + (1 - core) * (1 - 2 * x)) * 2 + core
    second = (y + (1 - core) * (1 - 2 * y)) * 4 + (x + core * (1 - 2 * x)) * 2 + core
    across = (1 - y) * 4 + (1 - x) * 2 + core
    flip = 1 - 2 * core
    sibling = me + flip

    barrier = pltpu.get_barrier_semaphore()
    for peer in (first, second, sibling):
        pl.semaphore_signal(barrier, inc=1, device_id=(peer, layer), device_id_type=MESH)
    for step in range(1, depth):
        pl.semaphore_signal(
            barrier, inc=1, device_id=(me, (layer + step) % depth), device_id_type=MESH
        )

    load_txt.wait()
    unit_txt, len_txt = normalize(raw_txt[...])
    col_in[layer] = jnp.concatenate([unit_txt[:, :half], unit_txt[:, half:]], axis=0).astype(
        BF16
    )
    load_img.wait()
    wide = raw_img[...].astype(F32)
    wide_img[...] = wide
    unit_all, _ = normalize(wide)
    img_buf[me] = unit_all.astype(BF16)

    pl.semaphore_wait(barrier, 2 + depth)

    started = []

    def push(src, dst, recv, device):
        copy = pltpu.make_async_remote_copy(
            src_ref=src,
            dst_ref=dst,
            send_sem=send_sem.at[len(started)],
            recv_sem=recv,
            device_id=device,
            device_id_type=MESH,
        )
        copy.start()
        started.append(copy)

    def part(buf, slot, chunk):
        return buf.at[slot, pl.ds(chunk * piece, piece)]

    def send(buf, slot, chunk, recv, *peers):
        for peer in peers:
            ref = part(buf, slot, chunk)
            push(ref, ref, recv.at[slot, chunk], (peer, layer))

    def landed(ref, recv):
        pltpu.make_async_remote_copy(
            src_ref=ref,
            dst_ref=ref,
            send_sem=send_sem.at[0],
            recv_sem=recv,
            device_id=(sibling, layer),
            device_id_type=MESH,
        ).wait_recv()

    def arrive(buf, slot, recv, *peers):
        for chunk in range(chunks):
            landed(part(buf, slot, chunk), recv.at[slot, chunk])
            send(buf, slot, chunk, recv, *peers)

    for step in range(1, depth):
        push(
            col_in.at[layer],
            col_in.at[layer],
            col_recv.at[layer],
            (me, (layer + step) % depth),
        )
    for chunk in range(chunks):
        send(img_buf, me, chunk, img_recv, first, second)
    for chunk in range(chunks):
        send(img_buf, me, chunk, img_recv, sibling)

    arrive(img_buf, first, img_recv, second, sibling)
    for step in range(1, depth):
        source = (layer + step) % depth
        landed(col_in.at[source], col_recv.at[source])
    pieces = []
    for z in range(depth):
        block = col_in[z].astype(F32)
        pieces.append(jnp.concatenate([block[:own], block[own:]], axis=1))
    txt_buf[me] = jnp.concatenate(pieces, axis=0).astype(BF16)
    for chunk in range(chunks):
        send(txt_buf, me, chunk, txt_recv, first, second)
    for chunk in range(chunks):
        send(txt_buf, me, chunk, txt_recv, sibling)

    arrive(img_buf, second, img_recv, sibling)
    arrive(img_buf, across, img_recv, sibling)
    arrive(txt_buf, first, txt_recv, second, sibling)
    for slot in (sibling, second + flip, first + flip, across + flip):
        arrive(img_buf, slot, img_recv)

    img_all = img_buf[...].reshape(total_rows, width)
    own_raw = wide_img[pl.ds(pl.multiple_of(layer * own, 8), own), :]
    own_img, len_img = normalize(own_raw)

    row_acc = jnp.zeros((8, total_rows), F32)
    row_sum = jnp.zeros((8, total_rows), F32)

    def absorb(start, count, row_acc, row_sum):
        block = txt_buf[pl.ds(start, count)].reshape(count * slot_rows, width)
        values = scaled_kernel(block, img_all)
        kt[pl.ds(start, count)] = values.reshape(count, slot_rows, total_rows)
        scale = 1.0 / jnp.sum(values, axis=1, keepdims=True)
        first_scale[pl.ds(start, count)] = scale.reshape(count, slot_rows, 1)
        return row_acc + fold_rows(values * scale), row_sum + fold_rows(values)

    arrive(txt_buf, sibling, txt_recv)
    row_acc, row_sum = absorb(me - core, 2, row_acc, row_sum)
    arrive(txt_buf, second, txt_recv, sibling)
    arrive(txt_buf, first + flip, txt_recv)
    row_acc, row_sum = absorb(first - core, 2, row_acc, row_sum)
    arrive(txt_buf, across, txt_recv, sibling)
    arrive(txt_buf, second + flip, txt_recv)
    row_acc, row_sum = absorb(second - core, 2, row_acc, row_sum)
    row_acc, row_sum = absorb(across, 1, row_acc, row_sum)
    arrive(txt_buf, across + flip, txt_recv)
    row_acc, row_sum = absorb(across + flip, 1, row_acc, row_sum)

    row_total = jnp.sum(row_sum, axis=0, keepdims=True)
    row_weight = 1.0 / jnp.sum(row_acc, axis=0, keepdims=True)
    previous = row_weight
    scales = []
    for step in range(1, ROUNDS):
        previous = row_weight
        row_acc = jnp.zeros((8, total_rows), F32)
        scales = []
        for slot in range(slots):
            scale = 1.0 / jnp.sum(kt[slot] * row_weight, axis=1, keepdims=True)
            row_acc += fold_rows(kt[slot] * scale)
            scales.append(scale)
        row_weight = 1.0 / jnp.sum(row_acc, axis=0, keepdims=True)

    keep = 1.0 - mix_weight
    lane = lax.broadcasted_iota(jnp.int32, (slot_rows, 128), 1)
    packed = []
    for slot in range(slots):
        last_cols = jnp.sum(kt[slot] * row_weight, axis=1, keepdims=True)
        weight = (keep + mix_weight * scales[slot] * last_cols) * first_scale[slot]
        packed.append(jnp.where(lane < 64, scales[slot], weight))
    packed = jnp.concatenate(packed, axis=0).T
    col_scale = packed[0:1]
    col_part = packed[64:65]

    at_row = lax.broadcasted_iota(jnp.int32, (own, total_rows), 0)
    at_col = lax.broadcasted_iota(jnp.int32, (own, total_rows), 1)

    def logit_grad(values, factor, place):
        eye = (at_col == at_row + place).astype(F32)
        return (0.5 * (values * factor - (2.0 * keep) * eye)).astype(BF16)

    values = scaled_kernel(unit_txt.astype(BF16), img_all)
    own_total = jnp.sum(values, axis=1, keepdims=True)
    own_scale = 1.0 / jnp.sum(values * previous, axis=1, keepdims=True)
    own_cols = jnp.sum(values * row_weight, axis=1, keepdims=True)
    own_part = (keep + mix_weight * own_scale * own_cols) / own_total
    factor = 1.0 / row_total + own_part - (2.0 * mix_weight) * (row_weight * own_scale)
    grad_logit = logit_grad(values, factor, layer * (slots * own) + me * own)
    g_txt = logit_scale * jnp.dot(grad_logit, img_all, preferred_element_type=F32)
    gtxt_ref[...] = project_back(g_txt, unit_txt, len_txt)

    txt_all = txt_buf[...].reshape(total_rows, width)
    values = scaled_kernel(own_img.astype(BF16), txt_all)
    own_total = jnp.sum(values, axis=1, keepdims=True)
    own_weight = 1.0 / jnp.sum(values * col_scale, axis=1, keepdims=True)
    group = me * depth + layer
    place = (group % slots) * slot_rows + (group // slots) * own
    factor = 1.0 / own_total + col_part - (2.0 * mix_weight) * (own_weight * col_scale)
    grad_logit = logit_grad(values, factor, place)
    g_img = logit_scale * jnp.dot(grad_logit, txt_all, preferred_element_type=F32)
    gimg_ref[...] = project_back(g_img, own_img, len_img)

    for copy in started:
        copy.wait_send()


def gathered(slots, depth, images, texts):
    slot_rows, width = images.shape
    own = texts.shape[0]
    total_rows = slots * slot_rows
    chunks = 2
    vmem = pl.BlockSpec(memory_space=pltpu.VMEM)
    anywhere = pl.BlockSpec(memory_space=pltpu.HBM)
    out = jax.ShapeDtypeStruct((own, width), F32)
    return pl.pallas_call(
        gathered_body,
        out_shape=(out, out),
        in_specs=[anywhere, anywhere],
        out_specs=(vmem, vmem),
        scratch_shapes=[
            pltpu.VMEM((slots, slot_rows, width), BF16),
            pltpu.VMEM((slots, slot_rows, width), BF16),
            pltpu.VMEM((depth, 2 * own, width // 2), BF16),
            pltpu.VMEM((slot_rows, width), F32),
            pltpu.VMEM((slot_rows, width), BF16),
            pltpu.VMEM((own, width), BF16),
            pltpu.VMEM((slots, slot_rows, total_rows), F32),
            pltpu.VMEM((slots, slot_rows, 1), F32),
            pltpu.SemaphoreType.DMA((depth - 1 + 14 * chunks,)),
            pltpu.SemaphoreType.DMA((slots, chunks)),
            pltpu.SemaphoreType.DMA((slots, chunks)),
            pltpu.SemaphoreType.DMA((depth,)),
            pltpu.SemaphoreType.DMA((2,)),
        ],
        compiler_params=pltpu.CompilerParams(
            collective_id=0, has_side_effects=True, vmem_limit_bytes=32 * 1024 * 1024
        ),
    )(images, texts)


def solution(mesh):
    placed = (P("img", None), P(("txt", "img"), None))
    slots, depth = mesh.shape["img"], mesh.shape["txt"]

    def body(images, texts):
        pairs = images.shape[0] * slots
        whole = slots == 8 and images.shape[0] % 32 == 0 and texts.shape[0] % 8 == 0
        if whole and pairs * pairs * 4 <= 4 * 1024 * 1024:
            return gathered(slots, depth, images, texts)
        return shards(images, texts)

    return jax.shard_map(
        body,
        mesh=mesh,
        in_specs=placed,
        out_specs=(P(("img", "txt"), None), P(("txt", "img"), None)),
        check_vma=False,
    )
```

profile of v0, /device:TPU:0, one launch (start us, length us, event | category | flops | bytes accessed | tf_op | source)
XLA Modules:
  0.0 24.1 jit_solution(9562818935018185987)
XLA Ops:
  0.6 0.0 copy-start
  0.6 0.9 %copy-done = bf16[96,512]{1,0:T(8,128)(2,1)S(1)} copy-done((bf16[96,512]{1,0:T(8,128)(2,1)S(1)}, bf16[96,512]{1,0:T(8,128)(2,1)}, u32[]{:S(2)}) %copy-start) | copy-done | bytes 98328
  1.5 0.0 copy-start.1
  1.5 0.7 %copy-done.1 = bf16[24,512]{1,0:T(8,128)(2,1)S(1)} copy-done((bf16[24,512]{1,0:T(8,128)(2,1)S(1)}, bf16[24,512]{1,0:T(8,128)(2,1)}, u32[]{:S(2)}) %copy-start.1) | copy-done | bytes 24600
  2.3 20.5 %shard_map.41 = (f32[24,512]{1,0:T(8,128)S(1)}, f32[24,512]{1,0:T(8,128)S(1)}) custom-call(bf16[96,512]{1,0:T(8,128)(2,1)S(1)} %copy-done, bf16[24,512]{1,0:T(8,128)(2,1)S(1)} %copy-done.1), custom_call_target="tpu_custom_call" | custom-call | tf_op jit(solution)/shard_map/pallas_call | solution.py:345
  22.8 0.6 %copy.6 = f32[24,512]{1,0:T(8,128)} copy(f32[24,512]{1,0:T(8,128)S(1)} %get-tuple-element.4) | data formatting | bytes 98304
  23.4 0.6 %copy.7 = f32[24,512]{1,0:T(8,128)} copy(f32[24,512]{1,0:T(8,128)S(1)} %get-tuple-element.5) | data formatting | bytes 98304
Async XLA Ops:
  0.6 0.9 %copy-start = (bf16[96,512]{1,0:T(8,128)(2,1)S(1)}, bf16[96,512]{1,0:T(8,128)(2,1)}, u32[]{:S(2)}) copy-start(bf16[96,512]{1,0:T(8,128)(2,1)} %images_ref.1) | copy-start | bytes 294916
  1.5 0.7 %copy-start.1 = (bf16[24,512]{1,0:T(8,128)(2,1)S(1)}, bf16[24,512]{1,0:T(8,128)(2,1)}, u32[]{:S(2)}) copy-start(bf16[24,512]{1,0:T(8,128)(2,1)} %texts_ref.1) | copy-start | bytes 73732
where the time goes:
time: 24.4 us; the launch traced here: 24.1 us
  Pallas kernels  20.5 us (84%)
  local copies, waits for them, and re-layouts  2.86 us (12%)
  between operations  0.65 us (3%)
    pallas_call x1, Pallas kernels, gathered(): pl.pallas_call(gathered_body, out_shape=(out, out), in_specs=[anywhere, a...  20.5 us
    unnamed x6, local copies, waits for them, and re-layouts  2.86 us

commit v1 on v0

--- a/solution.py
+++ b/solution.py
@@ -363,7 +363,7 @@
             pltpu.SemaphoreType.DMA((2,)),
         ],
         compiler_params=pltpu.CompilerParams(
-            collective_id=0, has_side_effects=True, vmem_limit_bytes=32 * 1024 * 1024
+            collective_id=0, has_side_effects=True, vmem_limit_bytes=60 * 1024 * 1024
         ),
     )(images, texts)
 

time: 24.4 us -> 24.1 us (0.988)
  local copies, waits for them, and re-layouts: 2.86 us -> 2.06 us
  Pallas kernels: 20.5 us -> 21.1 us
    unnamed x6 -> x4, local copies, waits for them, and re-layouts: 2.86 us -> 2.06 us
    pallas_call x1, Pallas kernels: 20.5 us -> 21.1 us  [gathered(): pl.pallas_call(gathered_body, out_shape=(out, out), in_specs=[anywhere, a...]
where the time goes in v1:
time: 24.1 us; the launch traced here: 23.8 us
  Pallas kernels  21.1 us (88%)
  local copies, waits for them, and re-layouts  2.06 us (9%)
  between operations  0.65 us (3%)
    pallas_call x1, Pallas kernels, gathered(): pl.pallas_call(gathered_body, out_shape=(out, out), in_specs=[anywhere, a...  21.1 us
    unnamed x4, local copies, waits for them, and re-layouts  2.06 us

profile of v1, /device:TPU:0, one launch (start us, length us, event | category | flops | bytes accessed | tf_op | source)
XLA Modules:
  0.0 23.8 jit_solution(7197662534713691979)
XLA Ops:
  0.6 21.1 %shard_map.41 = (f32[24,512]{1,0:T(8,128)}, f32[24,512]{1,0:T(8,128)}) custom-call(bf16[96,512]{1,0:T(8,128)(2,1)} %images_ref.1, bf16[24,512]{1,0:T(8,128)(2,1)} %texts_ref.1), custom_call_target="tpu_custom_call" | custom-call | tf_op jit(solution)/shard_map/pallas_call | solution.py:345
  21.7 0.0 copy-start
  21.7 1.4 %copy.6 = f32[24,512]{1,0:T(8,128)} copy(f32[24,512]{1,0:T(8,128)} %get-tuple-element.4) | data formatting | bytes 98304
  23.1 0.0 copy-done
  23.2 0.6 %copy.7 = f32[24,512]{1,0:T(8,128)} copy(f32[24,512]{1,0:T(8,128)S(1)} %copy-done) | data formatting | bytes 98304
Async XLA Ops:
  21.7 1.4 %copy-start = (f32[24,512]{1,0:T(8,128)S(1)}, f32[24,512]{1,0:T(8,128)}, u32[]{:S(2)}) copy-start(f32[24,512]{1,0:T(8,128)} %get-tuple-element.5) | copy-start | bytes 147460

commit v2 on v0

--- a/solution.py
+++ b/solution.py
@@ -173,12 +173,6 @@
     col_in[layer] = jnp.concatenate([unit_txt[:, :half], unit_txt[:, half:]], axis=0).astype(
         BF16
     )
-    load_img.wait()
-    wide = raw_img[...].astype(F32)
-    wide_img[...] = wide
-    unit_all, _ = normalize(wide)
-    img_buf[me] = unit_all.astype(BF16)
-
     pl.semaphore_wait(barrier, 2 + depth)
 
     started = []
@@ -225,10 +219,14 @@
             col_recv.at[layer],
             (me, (layer + step) % depth),
         )
+    load_img.wait()
     for chunk in range(chunks):
-        send(img_buf, me, chunk, img_recv, first, second)
-    for chunk in range(chunks):
-        send(img_buf, me, chunk, img_recv, sibling)
+        rows = pl.ds(chunk * piece, piece)
+        wide = raw_img[rows, :].astype(F32)
+        wide_img[rows, :] = wide
+        unit_part, _ = normalize(wide)
+        img_buf[me, rows] = unit_part.astype(BF16)
+        send(img_buf, me, chunk, img_recv, first, second, sibling)
 
     arrive(img_buf, first, img_recv, second, sibling)
     for step in range(1, depth):
@@ -365,7 +363,7 @@
         compiler_params=pltpu.CompilerParams(
             collective_id=0, has_side_effects=True, vmem_limit_bytes=32 * 1024 * 1024
         ),
-    )(images, texts)
+    )(*(pltpu.with_memory_space_constraint(array, pltpu.HBM) for array in (images, texts)))
 
 
 def solution(mesh):

time: 24.4 us -> 22.6 us (0.926)
  local copies, waits for them, and re-layouts: 2.86 us -> 1.24 us
    unnamed x6 -> x2, local copies, waits for them, and re-layouts: 2.86 us -> 1.24 us
where the time goes in v2:
time: 22.6 us; the launch traced here: 22.4 us
  Pallas kernels  20.5 us (91%)
  local copies, waits for them, and re-layouts  1.24 us (5%)
  between operations  0.64 us (3%)
    pallas_call x1, Pallas kernels, gathered(): pl.pallas_call(gathered_body, out_shape=(out, out), in_specs=[anywhere, a...  20.5 us
    unnamed x2, local copies, waits for them, and re-layouts  1.24 us

profile of v2, /device:TPU:0, one launch (start us, length us, event | category | flops | bytes accessed | tf_op | source)
XLA Modules:
  0.0 22.4 jit_solution(16629264462659827924)
XLA Ops:
  0.6 20.5 %shard_map.41 = (f32[24,512]{1,0:T(8,128)S(1)}, f32[24,512]{1,0:T(8,128)S(1)}) custom-call(bf16[96,512]{1,0:T(8,128)(2,1)} %images_ref.1, bf16[24,512]{1,0:T(8,128)(2,1)} %texts_ref.1), custom_call_target="tpu_custom_call" | custom-call | tf_op jit(solution)/shard_map/pallas_call | solution.py:343
  21.2 0.6 %copy.6 = f32[24,512]{1,0:T(8,128)} copy(f32[24,512]{1,0:T(8,128)S(1)} %get-tuple-element.4) | data formatting | bytes 98304
  21.8 0.6 %copy.7 = f32[24,512]{1,0:T(8,128)} copy(f32[24,512]{1,0:T(8,128)S(1)} %get-tuple-element.5) | data formatting | bytes 98304

commit v3 on v2

--- a/solution.py
+++ b/solution.py
@@ -121,8 +121,7 @@
 def gathered_body(
     images_ref,
     texts_ref,
-    gimg_ref,
-    gtxt_ref,
+    grad_ref,
     img_buf,
     txt_buf,
     col_in,
@@ -315,7 +314,7 @@
     factor = 1.0 / row_total + own_part - (2.0 * mix_weight) * (row_weight * own_scale)
     grad_logit = logit_grad(values, factor, layer * (slots * own) + me * own)
     g_txt = logit_scale * jnp.dot(grad_logit, img_all, preferred_element_type=F32)
-    gtxt_ref[...] = project_back(g_txt, unit_txt, len_txt)
+    grad_ref[own:] = project_back(g_txt, unit_txt, len_txt)
 
     txt_all = txt_buf[...].reshape(total_rows, width)
     values = scaled_kernel(own_img.astype(BF16), txt_all)
@@ -326,7 +325,7 @@
     factor = 1.0 / own_total + col_part - (2.0 * mix_weight) * (own_weight * col_scale)
     grad_logit = logit_grad(values, factor, place)
     g_img = logit_scale * jnp.dot(grad_logit, txt_all, preferred_element_type=F32)
-    gimg_ref[...] = project_back(g_img, own_img, len_img)
+    grad_ref[:own] = project_back(g_img, own_img, len_img)
 
     for copy in started:
         copy.wait_send()
@@ -336,15 +335,15 @@
     slot_rows, width = images.shape
     own = texts.shape[0]
     total_rows = slots * slot_rows
-    chunks = 2
+    chunks = 1
     vmem = pl.BlockSpec(memory_space=pltpu.VMEM)
     anywhere = pl.BlockSpec(memory_space=pltpu.HBM)
-    out = jax.ShapeDtypeStruct((own, width), F32)
-    return pl.pallas_call(
+    out = jax.ShapeDtypeStruct((2 * own, width), F32)
+    packed = pl.pallas_call(
         gathered_body,
-        out_shape=(out, out),
+        out_shape=out,
         in_specs=[anywhere, anywhere],
-        out_specs=(vmem, vmem),
+        out_specs=vmem,
         scratch_shapes=[
             pltpu.VMEM((slots, slot_rows, width), BF16),
             pltpu.VMEM((slots, slot_rows, width), BF16),
@@ -364,6 +363,7 @@
             collective_id=0, has_side_effects=True, vmem_limit_bytes=32 * 1024 * 1024
         ),
     )(*(pltpu.with_memory_space_constraint(array, pltpu.HBM) for array in (images, texts)))
+    return packed[:own], packed[own:]
 
 
 def solution(mesh):

time: 22.6 us -> 21.9 us (0.969)
  local copies, waits for them, and re-layouts: 1.24 us -> 0.64 us
    unnamed x2 -> x0, local copies, waits for them, and re-layouts: 1.24 us -> none
    slice x0 -> x1, local copies, waits for them, and re-layouts: none -> 0.64 us  [gathered(): return (packed[:own], packed[own:])]
where the time goes in v3:
time: 21.9 us; the launch traced here: 21.7 us
  Pallas kernels  20.4 us (93%)
  local copies, waits for them, and re-layouts  0.64 us (3%)
  between operations  0.64 us (3%)
    pallas_call x1, Pallas kernels, gathered(): pl.pallas_call(gathered_body, out_shape=out, in_specs=[anywhere, anywhere...  20.4 us
    slice x1, local copies, waits for them, and re-layouts, gathered(): return (packed[:own], packed[own:])  0.64 us

profile of v3, /device:TPU:0, one launch (start us, length us, event | category | flops | bytes accessed | tf_op | source)
XLA Modules:
  0.0 21.7 jit_solution(6886871775121822461)
XLA Ops:
  0.6 20.4 %shard_map.41 = f32[48,512]{1,0:T(8,128)S(1)} custom-call(bf16[96,512]{1,0:T(8,128)(2,1)} %images_ref.1, bf16[24,512]{1,0:T(8,128)(2,1)} %texts_ref.1), custom_call_target="tpu_custom_call" | custom-call | tf_op jit(solution)/shard_map/pallas_call | solution.py:342
  21.1 0.6 %fusion = (f32[24,512]{1,0:T(8,128)}, f32[24,512]{1,0:T(8,128)}) fusion(f32[48,512]{1,0:T(8,128)S(1)} %shard_map.41), kind=kLoop, calls=%fused_computation | loop fusion | bytes 196608 | tf_op jit(solution)/shard_map/slice | solution.py:366

commit v4 on v3

--- a/solution.py
+++ b/solution.py
@@ -103,14 +103,9 @@
 BF16 = jnp.bfloat16
 
 
-def nt_dot(left, right):
-    return lax.dot_general(
-        left, right, (((1,), (1,)), ((), ())), preferred_element_type=F32
-    )
-
-
 def scaled_kernel(left, right):
-    return jnp.exp(logit_scale * nt_dot(left, right) - logit_scale)
+    scores = jnp.dot(left, right, preferred_element_type=F32)
+    return jnp.exp(logit_scale * scores - logit_scale)
 
 
 def fold_rows(values):
@@ -130,6 +125,9 @@
     raw_txt,
     kt,
     first_scale,
+    img_turned,
+    own_turned,
+    own_scores,
     send_sem,
     img_recv,
     txt_recv,
@@ -250,13 +248,19 @@
     img_all = img_buf[...].reshape(total_rows, width)
     own_raw = wide_img[pl.ds(pl.multiple_of(layer * own, 8), own), :]
     own_img, len_img = normalize(own_raw)
+    img_turned[...] = img_all.T
+    padded = jnp.concatenate([own_img, jnp.zeros((128 - own, width), F32)], axis=0)
+    own_turned[...] = padded.T.astype(BF16)
 
     row_acc = jnp.zeros((8, total_rows), F32)
     row_sum = jnp.zeros((8, total_rows), F32)
 
     def absorb(start, count, row_acc, row_sum):
         block = txt_buf[pl.ds(start, count)].reshape(count * slot_rows, width)
-        values = scaled_kernel(block, img_all)
+        values = scaled_kernel(block, img_turned[...])
+        own_scores[pl.ds(start, count)] = jnp.dot(
+            block, own_turned[...], preferred_element_type=F32
+        ).reshape(count, slot_rows, 128)
         kt[pl.ds(start, count)] = values.reshape(count, slot_rows, total_rows)
         scale = 1.0 / jnp.sum(values, axis=1, keepdims=True)
         first_scale[pl.ds(start, count)] = scale.reshape(count, slot_rows, 1)
@@ -306,7 +310,7 @@
         eye = (at_col == at_row + place).astype(F32)
         return (0.5 * (values * factor - (2.0 * keep) * eye)).astype(BF16)
 
-    values = scaled_kernel(unit_txt.astype(BF16), img_all)
+    values = scaled_kernel(unit_txt.astype(BF16), img_turned[...])
     own_total = jnp.sum(values, axis=1, keepdims=True)
     own_scale = 1.0 / jnp.sum(values * previous, axis=1, keepdims=True)
     own_cols = jnp.sum(values * row_weight, axis=1, keepdims=True)
@@ -317,7 +321,8 @@
     grad_ref[own:] = project_back(g_txt, unit_txt, len_txt)
 
     txt_all = txt_buf[...].reshape(total_rows, width)
-    values = scaled_kernel(own_img.astype(BF16), txt_all)
+    scores = own_scores[...].reshape(total_rows, 128).T[:own]
+    values = jnp.exp(logit_scale * scores - logit_scale)
     own_total = jnp.sum(values, axis=1, keepdims=True)
     own_weight = 1.0 / jnp.sum(values * col_scale, axis=1, keepdims=True)
     group = me * depth + layer
@@ -353,6 +358,9 @@
             pltpu.VMEM((own, width), BF16),
             pltpu.VMEM((slots, slot_rows, total_rows), F32),
             pltpu.VMEM((slots, slot_rows, 1), F32),
+            pltpu.VMEM((width, total_rows), BF16),
+            pltpu.VMEM((width, 128), BF16),
+            pltpu.VMEM((slots, slot_rows, 128), F32),
             pltpu.SemaphoreType.DMA((depth - 1 + 14 * chunks,)),
             pltpu.SemaphoreType.DMA((slots, chunks)),
             pltpu.SemaphoreType.DMA((slots, chunks)),

time: 21.9 us -> 21.5 us (0.982)
  Pallas kernels: 20.4 us -> 19.9 us
    pallas_call x1, Pallas kernels: 20.4 us -> 19.9 us  [gathered(): pl.pallas_call(gathered_body, out_shape=out, in_specs=[anywhere, anywhere...]
where the time goes in v4:
time: 21.5 us; the launch traced here: 21.2 us
  Pallas kernels  19.9 us (93%)
  local copies, waits for them, and re-layouts  0.64 us (3%)
  between operations  0.64 us (3%)
    pallas_call x1, Pallas kernels, gathered(): pl.pallas_call(gathered_body, out_shape=out, in_specs=[anywhere, anywhere...  19.9 us
    slice x1, local copies, waits for them, and re-layouts, gathered(): return (packed[:own], packed[own:])  0.64 us

profile of v4, /device:TPU:0, one launch (start us, length us, event | category | flops | bytes accessed | tf_op | source)
XLA Modules:
  0.0 21.2 jit_solution(17315616196982591434)
XLA Ops:
  0.6 19.9 %shard_map.41 = f32[48,512]{1,0:T(8,128)S(1)} custom-call(bf16[96,512]{1,0:T(8,128)(2,1)} %images_ref.1, bf16[24,512]{1,0:T(8,128)(2,1)} %texts_ref.1), custom_call_target="tpu_custom_call" | custom-call | tf_op jit(solution)/shard_map/pallas_call | solution.py:347
  20.6 0.6 %fusion = (f32[24,512]{1,0:T(8,128)}, f32[24,512]{1,0:T(8,128)}) fusion(f32[48,512]{1,0:T(8,128)S(1)} %shard_map.41), kind=kLoop, calls=%fused_computation | loop fusion | bytes 196608 | tf_op jit(solution)/shard_map/slice | solution.py:374

commit v5 on v4

--- a/solution.py
+++ b/solution.py
@@ -101,11 +101,15 @@
 MESH = pl.DeviceIdType.MESH
 F32 = jnp.float32
 BF16 = jnp.bfloat16
+power_scale = logit_scale * 1.4426950408889634
+
+
+def shifted_exp(scores):
+    return jnp.exp2(scores * power_scale - power_scale)
 
 
 def scaled_kernel(left, right):
-    scores = jnp.dot(left, right, preferred_element_type=F32)
-    return jnp.exp(logit_scale * scores - logit_scale)
+    return shifted_exp(jnp.dot(left, right, preferred_element_type=F32))
 
 
 def fold_rows(values):
@@ -186,6 +190,14 @@
         copy.start()
         started.append(copy)
 
+    settled = []
+
+    def settle(index):
+        index = index % len(started)
+        for copy in started[index : index + 2 * chunks : 2]:
+            copy.wait_send()
+            settled.append(copy)
+
     def part(buf, slot, chunk):
         return buf.at[slot, pl.ds(chunk * piece, piece)]
 
@@ -223,7 +235,10 @@
         wide_img[rows, :] = wide
         unit_part, _ = normalize(wide)
         img_buf[me, rows] = unit_part.astype(BF16)
-        send(img_buf, me, chunk, img_recv, first, second, sibling)
+        send(img_buf, me, chunk, img_recv, first, sibling)
+    settle(-2 * chunks)
+    for chunk in range(chunks):
+        send(img_buf, me, chunk, img_recv, second)
 
     arrive(img_buf, first, img_recv, second, sibling)
     for step in range(1, depth):
@@ -235,12 +250,14 @@
         pieces.append(jnp.concatenate([block[:own], block[own:]], axis=1))
     txt_buf[me] = jnp.concatenate(pieces, axis=0).astype(BF16)
     for chunk in range(chunks):
-        send(txt_buf, me, chunk, txt_recv, first, second)
-    for chunk in range(chunks):
-        send(txt_buf, me, chunk, txt_recv, sibling)
+        send(txt_buf, me, chunk, txt_recv, first, sibling)
+    text_start = len(started) - 2 * chunks
 
     arrive(img_buf, second, img_recv, sibling)
     arrive(img_buf, across, img_recv, sibling)
+    settle(text_start)
+    for chunk in range(chunks):
+        send(txt_buf, me, chunk, txt_recv, second)
     arrive(txt_buf, first, txt_recv, second, sibling)
     for slot in (sibling, second + flip, first + flip, across + flip):
         arrive(img_buf, slot, img_recv)
@@ -322,7 +339,7 @@
 
     txt_all = txt_buf[...].reshape(total_rows, width)
     scores = own_scores[...].reshape(total_rows, 128).T[:own]
-    values = jnp.exp(logit_scale * scores - logit_scale)
+    values = shifted_exp(scores)
     own_total = jnp.sum(values, axis=1, keepdims=True)
     own_weight = 1.0 / jnp.sum(values * col_scale, axis=1, keepdims=True)
     group = me * depth + layer
@@ -333,7 +350,8 @@
     grad_ref[:own] = project_back(g_img, own_img, len_img)
 
     for copy in started:
-        copy.wait_send()
+        if not any(copy is other for other in settled):
+            copy.wait_send()
 
 
 def gathered(slots, depth, images, texts):

time: 21.5 us -> 23.5 us (1.093)
  Pallas kernels: 19.9 us -> 22.1 us
    pallas_call x1, Pallas kernels: 19.9 us -> 22.1 us  [gathered(): pl.pallas_call(gathered_body, out_shape=out, in_specs=[anywhere, anywhere...]
where the time goes in v5:
time: 23.5 us; the launch traced here: 23.3 us
  Pallas kernels  22.1 us (94%)
  local copies, waits for them, and re-layouts  0.64 us (3%)
  between operations  0.64 us (3%)
    pallas_call x1, Pallas kernels, gathered(): pl.pallas_call(gathered_body, out_shape=out, in_specs=[anywhere, anywhere...  22.1 us
    slice x1, local copies, waits for them, and re-layouts, gathered(): return (packed[:own], packed[own:])  0.64 us

profile of v5, /device:TPU:0, one launch (start us, length us, event | category | flops | bytes accessed | tf_op | source)
XLA Modules:
  0.0 23.3 jit_solution(11274157780775009103)
XLA Ops:
  0.6 22.1 %shard_map.41 = f32[48,512]{1,0:T(8,128)S(1)} custom-call(bf16[96,512]{1,0:T(8,128)(2,1)} %images_ref.1, bf16[24,512]{1,0:T(8,128)(2,1)} %texts_ref.1), custom_call_target="tpu_custom_call" | custom-call | tf_op jit(solution)/shard_map/pallas_call | solution.py:365
  22.7 0.6 %fusion = (f32[24,512]{1,0:T(8,128)}, f32[24,512]{1,0:T(8,128)}) fusion(f32[48,512]{1,0:T(8,128)S(1)} %shard_map.41), kind=kLoop, calls=%fused_computation | loop fusion | bytes 196608 | tf_op jit(solution)/shard_map/slice | solution.py:392

commit v6 on v4

--- a/solution.py
+++ b/solution.py
@@ -101,11 +101,15 @@
 MESH = pl.DeviceIdType.MESH
 F32 = jnp.float32
 BF16 = jnp.bfloat16
+power_scale = logit_scale * 1.4426950408889634
+
+
+def shifted_exp(scores):
+    return jnp.exp2(scores * power_scale - power_scale)
 
 
 def scaled_kernel(left, right):
-    scores = jnp.dot(left, right, preferred_element_type=F32)
-    return jnp.exp(logit_scale * scores - logit_scale)
+    return shifted_exp(jnp.dot(left, right, preferred_element_type=F32))
 
 
 def fold_rows(values):
@@ -225,7 +229,13 @@
         img_buf[me, rows] = unit_part.astype(BF16)
         send(img_buf, me, chunk, img_recv, first, second, sibling)
 
+    own_raw = wide_img[pl.ds(pl.multiple_of(layer * own, 8), own), :]
+    own_img, len_img = normalize(own_raw)
+    padded = jnp.concatenate([own_img, jnp.zeros((128 - own, width), F32)], axis=0)
+    own_turned[...] = padded.T.astype(BF16)
+
     arrive(img_buf, first, img_recv, second, sibling)
+    arrive(img_buf, second, img_recv, sibling)
     for step in range(1, depth):
         source = (layer + step) % depth
         landed(col_in.at[source], col_recv.at[source])
@@ -239,18 +249,13 @@
     for chunk in range(chunks):
         send(txt_buf, me, chunk, txt_recv, sibling)
 
-    arrive(img_buf, second, img_recv, sibling)
     arrive(img_buf, across, img_recv, sibling)
     arrive(txt_buf, first, txt_recv, second, sibling)
     for slot in (sibling, second + flip, first + flip, across + flip):
         arrive(img_buf, slot, img_recv)
 
     img_all = img_buf[...].reshape(total_rows, width)
-    own_raw = wide_img[pl.ds(pl.multiple_of(layer * own, 8), own), :]
-    own_img, len_img = normalize(own_raw)
     img_turned[...] = img_all.T
-    padded = jnp.concatenate([own_img, jnp.zeros((128 - own, width), F32)], axis=0)
-    own_turned[...] = padded.T.astype(BF16)
 
     row_acc = jnp.zeros((8, total_rows), F32)
     row_sum = jnp.zeros((8, total_rows), F32)
@@ -322,7 +327,7 @@
 
     txt_all = txt_buf[...].reshape(total_rows, width)
     scores = own_scores[...].reshape(total_rows, 128).T[:own]
-    values = jnp.exp(logit_scale * scores - logit_scale)
+    values = shifted_exp(scores)
     own_total = jnp.sum(values, axis=1, keepdims=True)
     own_weight = 1.0 / jnp.sum(values * col_scale, axis=1, keepdims=True)
     group = me * depth + layer

time: 21.5 us -> 21.6 us (level)
  Pallas kernels: 19.9 us -> 20.2 us
    pallas_call x1, Pallas kernels: 19.9 us -> 20.2 us  [gathered(): pl.pallas_call(gathered_body, out_shape=out, in_specs=[anywhere, anywhere...]
where the time goes in v6:
time: 21.6 us; the launch traced here: 21.5 us
  Pallas kernels  20.2 us (94%)
  local copies, waits for them, and re-layouts  0.64 us (3%)
  between operations  0.64 us (3%)
    pallas_call x1, Pallas kernels, gathered(): pl.pallas_call(gathered_body, out_shape=out, in_specs=[anywhere, anywhere...  20.2 us
    slice x1, local copies, waits for them, and re-layouts, gathered(): return (packed[:own], packed[own:])  0.64 us

profile of v6, /device:TPU:0, one launch (start us, length us, event | category | flops | bytes accessed | tf_op | source)
XLA Modules:
  0.0 21.5 jit_solution(4979171647696462577)
XLA Ops:
  0.6 20.2 %shard_map.41 = f32[48,512]{1,0:T(8,128)S(1)} custom-call(bf16[96,512]{1,0:T(8,128)(2,1)} %images_ref.1, bf16[24,512]{1,0:T(8,128)(2,1)} %texts_ref.1), custom_call_target="tpu_custom_call" | custom-call | tf_op jit(solution)/shard_map/pallas_call | solution.py:352
  20.9 0.6 %fusion = (f32[24,512]{1,0:T(8,128)}, f32[24,512]{1,0:T(8,128)}) fusion(f32[48,512]{1,0:T(8,128)S(1)} %shard_map.41), kind=kLoop, calls=%fused_computation | loop fusion | bytes 196608 | tf_op jit(solution)/shard_map/slice | solution.py:379

commit v7 on v6

--- a/solution.py
+++ b/solution.py
@@ -279,9 +279,8 @@
     arrive(txt_buf, across, txt_recv, sibling)
     arrive(txt_buf, second + flip, txt_recv)
     row_acc, row_sum = absorb(second - core, 2, row_acc, row_sum)
-    row_acc, row_sum = absorb(across, 1, row_acc, row_sum)
     arrive(txt_buf, across + flip, txt_recv)
-    row_acc, row_sum = absorb(across + flip, 1, row_acc, row_sum)
+    row_acc, row_sum = absorb(across - core, 2, row_acc, row_sum)
 
     row_total = jnp.sum(row_sum, axis=0, keepdims=True)
     row_weight = 1.0 / jnp.sum(row_acc, axis=0, keepdims=True)

time: 21.6 us -> 21.8 us (level)
  no operation moved by 1% of the time
where the time goes in v7:
time: 21.8 us; the launch traced here: 21.6 us
  Pallas kernels  20.3 us (93%)
  local copies, waits for them, and re-layouts  0.64 us (3%)
  between operations  0.64 us (3%)
    pallas_call x1, Pallas kernels, gathered(): pl.pallas_call(gathered_body, out_shape=out, in_specs=[anywhere, anywhere...  20.3 us
    slice x1, local copies, waits for them, and re-layouts, gathered(): return (packed[:own], packed[own:])  0.64 us

profile of v7, /device:TPU:0, one launch (start us, length us, event | category | flops | bytes accessed | tf_op | source)
XLA Modules:
  0.0 21.6 jit_solution(9380935896360338555)
XLA Ops:
  0.6 20.3 %shard_map.41 = f32[48,512]{1,0:T(8,128)S(1)} custom-call(bf16[96,512]{1,0:T(8,128)(2,1)} %images_ref.1, bf16[24,512]{1,0:T(8,128)(2,1)} %texts_ref.1), custom_call_target="tpu_custom_call" | custom-call | tf_op jit(solution)/shard_map/pallas_call | solution.py:351
  21.0 0.6 %fusion = (f32[24,512]{1,0:T(8,128)}, f32[24,512]{1,0:T(8,128)}) fusion(f32[48,512]{1,0:T(8,128)S(1)} %shard_map.41), kind=kLoop, calls=%fused_computation | loop fusion | bytes 196608 | tf_op jit(solution)/shard_map/slice | solution.py:378
